TPU v7x, 256 devices: a whole 4x4x8 slice. The times are simulated.
256 devices in a mesh: dp: 64 (over z, y, core), mp: 4 (over x).
Axes of the slice: x: 4, y: 4, z: 8, core: 2. Of those that a mesh axis runs over, the one named last changes fastest.
Arguments:
- last_query: bfloat16 [2048, 4096], P('dp', 'mp'), may hold values from -6 to 6
- key_cache: bfloat16 [131072, 1024], P('dp', 'mp'), may hold values from -6 to 6
- value_cache: bfloat16 [131072, 1024], P('dp', 'mp'), may hold values from -6 to 6
- residual: bfloat16 [2048, 4096], P('dp', 'mp'), may hold values from -6 to 6
- out_weight: bfloat16 [4096, 4096], P('mp'), may hold values from -0.09375 to 0.09375
- query_emb: bfloat16 [2048, 4096], P('dp', 'mp'), may hold values from -1 to 1
- lengths: int32 [64, 32], P('dp'), may hold values from 1 to 256, 2048 in all within a row
- positives: int32 [2048], P('dp'), may hold values from 0 to 2047, each once
Outputs:
- query_loss: float32 [2048], P('dp')
- query_grad: float32 [2048, 4096], P('dp', 'mp')
- residual_grad: float32 [2048, 4096], P('dp', 'mp')
- lastq_grad: float32 [2048, 4096], P('dp', 'mp')
- key_grad: bfloat16 [131072, 1024], P('dp', 'mp')
- value_grad: bfloat16 [131072, 1024], P('dp', 'mp')
Inputs may be any that keep to these rules, and one draw needn't show every extreme that they name: Each row of lengths sums to 2048; its largest entry is 256. `positives`: each passage is the positive of exactly one query.
All inputs are finite; a program needn't handle non-finite values.
Results may differ from a plain program's by a relative error of at most 0.029.
Values may be sent and summed in bfloat16 or wider, within the bound.
A program may use at most 128 MiB of HBM per device.

v0:
```python
import functools

import jax
import jax.numpy as jnp
from jax import lax
from jax.experimental import pallas as pl
from jax.experimental.pallas import tpu as pltpu
from jax.sharding import PartitionSpec as P

HEAD_DIM = 128
INV_TEMP = 50.0
EPSILON = 1e-06
CORES = 2
MESH = pl.DeviceIdType.MESH
F32 = jnp.float32
BF16 = jnp.bfloat16


def dot_nn(a, b):
    return lax.dot_general(a, b, (((1,), (0,)), ((), ())), preferred_element_type=F32)


def dot_nt(a, b):
    return lax.dot_general(a, b, (((1,), (1,)), ((), ())), preferred_element_type=F32)


def dot_tn(a, b):
    return lax.dot_general(a, b, (((0,), (0,)), ((), ())), preferred_element_type=F32)


def kernel(
    sizes,
    lastq_hbm, key_hbm, value_hbm, resid_hbm, weight_hbm, query_hbm, len_ref, pos_ref,
    loss_hbm, qgrad_hbm, rgrad_hbm, up_hbm, out_hbm, probs_hbm,
    q_buf, p_buf, weight, key, value, lastq, resid, ranges, attn, probs, y_part, y_recv, s_part, s_recv, sq_all, turned,
    stat, s_all, w_all, misc_all, eg_part, eg_own, eg_side, eg_out, eg_recv, slope_all, qg_part, qg_recv,
    relay, relay_half, loss_ref, qgrad_ref, rgrad_ref, up_ref, out_ref,
    load_sem, save_sem, send_sem, recv_sem,
):
    nz, ny, nx = sizes
    rows, width = query_hbm.shape
    tokens, kv_width = key_hbm.shape
    groups = kv_width // HEAD_DIM
    heads = width // kv_width
    inner = CORES * ny
    passages = inner * rows
    slots = nz // nx
    chunk = slots * rows
    scale = 1.0 / HEAD_DIM**0.5

    me = lax.axis_index("dp")
    x = lax.axis_index("mp")
    core = lax.rem(me, CORES)
    y = lax.rem(lax.div(me, CORES), ny)
    z = lax.div(me, inner)

    def place(z_at, y_at, core_at):
        return {"dp": (z_at * ny + y_at) * CORES + core_at}

    def around(at, step, size):
        return lax.rem(at + (step + size), size)

    def far_first(size):
        return sorted(range(1, size), key=lambda k: -min(k, size - k))

    xs = [around(x, k, nx) for k in range(nx)]
    ys = [around(y, k, ny) for k in range(ny)]
    zs = [around(z, k, nz) for k in range(nz)]
    twin = place(z, y, 1 - core)
    partners = [place(t, y, core) for t in zs[1:]] + [place(z, t, core) for t in ys[1:]]
    partners += [twin] + [{"mp": t} for t in xs[1:]]

    barrier = pltpu.get_barrier_semaphore()
    for partner in partners:
        pl.semaphore_signal(barrier, inc=1, device_id=partner, device_id_type=MESH)

    loads = [
        pltpu.make_async_copy(query_hbm, q_buf.at[z, :, pl.ds(0, width)], load_sem.at[0]),
        pltpu.make_async_copy(lastq_hbm, lastq, load_sem.at[1]),
        pltpu.make_async_copy(key_hbm, key, load_sem.at[2]),
        pltpu.make_async_copy(value_hbm, value, load_sem.at[3]),
        pltpu.make_async_copy(resid_hbm, resid, load_sem.at[4]),
    ]
    waits = {}
    for k in far_first(nx) + [0]:
        waits[k] = len(loads)
        columns = pl.ds(pl.multiple_of(xs[k] * width, width), width)
        loads.append(
            pltpu.make_async_copy(weight_hbm.at[:, columns], weight.at[k], load_sem.at[5 + k])
        )
    for load in loads[:4]:
        load.start()

    saves = []

    def save(source, target):
        saves.append(pltpu.make_async_copy(source, target, save_sem.at[len(saves)]))
        saves[-1].start()

    sent = []

    def push(src, dst, device):
        index = len(sent)
        copy = pltpu.make_async_remote_copy(
            src_ref=src,
            dst_ref=dst,
            send_sem=send_sem.at[index],
            recv_sem=recv_sem.at[index],
            device_id=device,
            device_id_type=MESH,
        )
        copy.start()
        sent.append(copy)
        return copy

    def exchange(src, dst):
        copies = [None] * nx
        for k in far_first(nx):
            copies[k] = push(src(k), dst.at[x], {"mp": xs[k]})
        return copies

    def received(copies, k):
        copies[k].wait_recv()
        return xs[nx - k]

    lane = lax.broadcasted_iota(jnp.int32, (rows, HEAD_DIM), 1)

    def three_parts(column):
        high = column.astype(BF16).astype(F32)
        middle = (column - high).astype(BF16).astype(F32)
        low = column - high - middle
        parts = jnp.where(lane == 0, high, jnp.where(lane == 1, middle, low))
        return jnp.where(lane < 3, parts, 0.0).astype(BF16)

    position = jnp.broadcast_to(pos_ref[...].astype(F32), (rows, rows))
    diagonal = lax.broadcasted_iota(jnp.int32, (rows, rows), 0) == lax.broadcasted_iota(
        jnp.int32, (rows, rows), 1
    )
    position = jnp.sum(jnp.where(diagonal, position, 0.0), axis=1, keepdims=True).astype(jnp.int32)
    high, low = lax.shift_right_logical(position, 6), position & 63
    digits = jnp.where(lane == 0, high, jnp.where(lane == 1, low, 0)).astype(F32).astype(BF16)
    q_buf[z, :, width:] = digits
    lengths = len_ref[...].astype(F32)
    passage = lax.broadcasted_iota(jnp.int32, (rows, rows), 0)
    which = lax.broadcasted_iota(jnp.int32, (rows, rows), 1)
    for i, before in enumerate((which < passage, which <= passage)):
        bound = jnp.sum(jnp.where(before, lengths, 0.0), axis=1, keepdims=True)
        ranges[i] = jnp.broadcast_to(bound, (rows, HEAD_DIM)).astype(jnp.int32)
    loads[0].wait()
    pl.semaphore_wait(barrier, len(partners))
    q_copies = {
        k: push(q_buf.at[z], q_buf.at[z], place(zs[k], y, core)) for k in (2, nz - 2, 1, nz - 1)
    }

    block = 16

    def softmax_rows(i, carry):
        at = pl.ds(pl.multiple_of(i * block, block), block)
        bounds = pl.ds(pl.multiple_of(lax.rem(i, rows // block) * block, block), block)
        token = lax.broadcasted_iota(jnp.int32, (block, tokens), 1)
        inside = (token >= ranges[0, bounds, :][:, :1]) & (token < ranges[1, bounds, :][:, :1])
        scores = jnp.where(inside, attn[at, :], -1e30)
        top = jnp.max(scores, axis=1, keepdims=True)
        powers = jnp.exp((scores - top) * scale)
        weights = powers * (1.0 / jnp.sum(powers, axis=1, keepdims=True))
        probs[at, :] = weights.astype(BF16)
        return carry

    for load in loads[1:4]:
        load.wait()
    for load in loads[4:]:
        load.start()
    group_rows = heads * rows
    blocks = groups * group_rows // block
    attn[...] = dot_nt(spread(lastq, groups, heads), key[...])
    lax.fori_loop(0, blocks, softmax_rows, 0, unroll=blocks)
    out = dot_nn(probs[...], value[...])
    attended = [
        out[g * group_rows + h * rows : g * group_rows + (h + 1) * rows, g * HEAD_DIM :][:, :HEAD_DIM]
        for g in range(groups)
        for h in range(heads)
    ]
    attended = jnp.concatenate(attended, axis=1)
    out_ref[...] = attended
    attended = attended.astype(BF16)

    side_width = width // 2
    sides = [slice(i * side_width, (i + 1) * side_width) for i in range(2)]

    def project(k, i):
        if i == 0:
            loads[waits[k]].wait()
        y_part[k, :, sides[i]] = dot_nn(attended, weight[k, :, sides[i]]).astype(BF16)
        return y_part.at[k, :, pl.ds(i * side_width, side_width)]

    y_copies = []
    for i in range(2):
        target = y_recv.at[:, :, pl.ds(i * side_width, side_width)]
        y_copies.append(exchange(lambda k: project(k, i), target))
    save(probs, probs_hbm)
    save(out_ref, out_hbm)
    loads[4].wait()
    loads[waits[0]].wait()
    hiddens = [
        dot_nn(attended, weight[0, :, part]) + resid[:, part].astype(F32) for part in sides
    ]
    half = rows // 2
    onward = []
    for k, first in ((2, 0), (nz - 2, half)):
        q_copies[k].wait_recv()
        step = 1 if k == 2 else nz - 1
        part = q_buf.at[zs[nz - k]]
        onward.append(push(part, part, place(zs[step], y, core)))
        part = q_buf.at[zs[nz - k], pl.ds(first, half)]
        onward.append(push(part, part, place(zs[k], y, core)))

    own = core * ny + y
    spans = (pl.ds(0, side_width), pl.ds(side_width, side_width + HEAD_DIM))
    p_copies = [[None] * ny, [None] * ny]
    passed = [[], []]
    for i, part in enumerate(sides):
        for k in range(1, nx):
            t = received(y_copies[i], k)
            hiddens[i] = hiddens[i] + y_recv[t, :, part].astype(F32)
        p_buf[own, :, part] = hiddens[i].astype(BF16)
        if i == 1:
            squares = [jnp.sum(hidden * hidden, axis=1, keepdims=True) for hidden in hiddens]
            p_buf[own, :, width:] = three_parts(squares[0] + squares[1])
        block_at = p_buf.at[own, :, spans[i]]
        for k in far_first(ny):
            p_copies[i][k] = push(block_at, block_at, place(z, ys[k], core))
        passed[i].append(push(block_at, block_at, twin))
    for i in range(2):
        for k in sorted(range(1, ny), key=lambda k: min(k, ny - k)):
            p_copies[i][k].wait_recv()
            block_at = p_buf.at[core * ny + ys[ny - k], :, spans[i]]
            passed[i].append(push(block_at, block_at, twin))
    for copy in [q_copies[1], q_copies[nz - 1]] + onward:
        copy.wait_recv()

    def partial_scores(t, i):
        part = q_buf[pl.ds(t * slots, slots), :, sides[i]].reshape(chunk, side_width)
        return dot_nt(part, p_buf[:, :, sides[i]].reshape(passages, side_width))

    for copy in passed[0]:
        copy.wait_recv()
    for k in range(nx):
        s_part[k] = partial_scores(xs[k], 0)
    for copy in passed[1]:
        copy.wait_recv()

    def send_scores(k):
        s_part[k] += partial_scores(xs[k], 1)
        return s_part.at[k]

    unit = (lax.broadcasted_iota(jnp.int32, (8, HEAD_DIM), 1) < 3).astype(F32).astype(BF16)
    sq_all[x] = dot_nt(unit, p_buf[:, :, width:].reshape(passages, HEAD_DIM))
    sq_copies = exchange(lambda k: sq_all.at[x], sq_all)
    s_copies = exchange(send_scores, s_recv)
    scores = s_part[0] + partial_scores(x, 1)
    squares = sq_all[x]
    for k in range(1, nx):
        squares = squares + sq_all[received(sq_copies, k)]
    norms = jnp.sqrt(squares[:1] + EPSILON)
    turned[...] = jnp.broadcast_to(norms, (HEAD_DIM, passages)).T
    norm = turned[pl.ds(pl.multiple_of(own * rows, rows), rows), :][:, :1]
    embs = [hidden / norm for hidden in hiddens]
    digits = q_buf[:, :, width:].reshape(nz * rows, HEAD_DIM).astype(F32)
    positive = (digits[:, 0:1] * 64.0 + digits[:, 1:2]).astype(jnp.int32)
    index = lax.broadcasted_iota(jnp.int32, (nz * rows, passages), 1)
    slot = lax.div(index, rows)
    cell = lax.rem(slot, ny) * CORES + lax.div(slot, ny)
    passage_of = (z * inner + cell) * rows + lax.rem(index, rows)
    match = positive == passage_of
    for k in range(1, nx):
        scores = scores + s_recv[received(s_copies, k)]
    scores = scores * (INV_TEMP / norms)
    s_all[x] = scores
    all_copies = exchange(lambda k: s_all.at[x], s_all)

    top = jnp.max(scores, axis=1, keepdims=True)
    total = jnp.sum(jnp.exp(scores - top), axis=1, keepdims=True)
    own_digits = q_buf[pl.ds(x * slots, slots), :, width:].reshape(chunk, HEAD_DIM).astype(F32)
    own_positive = (own_digits[:, 0:1] * 64.0 + own_digits[:, 1:2]).astype(jnp.int32)
    own_match = own_positive == passage_of[:chunk]
    hit = jnp.sum(jnp.where(own_match, scores, 0.0), axis=1, keepdims=True)
    chunk_lane = lax.broadcasted_iota(jnp.int32, (chunk, HEAD_DIM), 1)
    columns = jnp.where(chunk_lane == 0, top, jnp.where(chunk_lane == 1, total, hit))
    stat[z] = jnp.concatenate([columns] * (HEAD_DIM // chunk), axis=0).T[:8]
    stat_copies = [push(stat.at[z], stat.at[z], place(zs[k], y, core)) for k in far_first(nz)]
    for copy in stat_copies:
        copy.wait_recv()
    every = stat[...]
    top = jnp.max(every[:, 0:1], axis=0)
    total = jnp.sum(every[:, 1:2] * jnp.exp(every[:, 0:1] - top[None]), axis=0)
    lse = top + jnp.log(total)
    loss = lse - jnp.sum(every[:, 2:3], axis=0)
    line = lax.broadcasted_iota(jnp.int32, (8, HEAD_DIM), 0)
    misc_all[x] = jnp.where(line == 0, lse, loss)
    misc_copies = exchange(lambda k: misc_all.at[x], misc_all)
    for k in range(1, nx):
        received(all_copies, k)
    for k in range(1, nx):
        received(misc_copies, k)
    losses = misc_all[lax.div(z, slots)][1:2]
    own_loss = losses[:, :rows]
    for k in range(1, slots):
        own_loss = jnp.where(lax.rem(z, slots) == k, losses[:, k * rows : (k + 1) * rows], own_loss)
    loss_ref[...] = own_loss
    save(loss_ref, loss_hbm)

    lines = [misc_all[t][:1] for t in range(nx)] + [jnp.zeros((HEAD_DIM - nx, HEAD_DIM), F32)]
    turned_lse = jnp.concatenate(lines, axis=0).T
    lse = jnp.concatenate([turned_lse[:chunk, t : t + 1] for t in range(nx)], axis=0)
    scores = s_all[...].reshape(nx * chunk, passages)
    pairs = jnp.exp(scores - lse) - match.astype(F32)
    along = jnp.sum(pairs.astype(BF16).astype(F32) * scores, axis=0, keepdims=True)
    w_all[...] = pairs.astype(BF16)
    turned[...] = jnp.broadcast_to(along, (HEAD_DIM, passages)).T

    share = ny * rows
    spans = ((0, HEAD_DIM + side_width), (HEAD_DIM + side_width, side_width))

    def emb_share(core_at, i):
        part = w_all[:, pl.ds(pl.multiple_of(core_at * share, share), share)]
        queries = q_buf[:, :, i * side_width : (i + 1) * side_width].reshape(nz * rows, side_width)
        return (dot_tn(part, queries) * INV_TEMP).reshape(ny, rows, side_width)

    def along_of(core_at, y_at):
        first = pl.multiple_of((core_at * ny + y_at) * rows, rows)
        return turned[pl.ds(first, rows), :][:, :1]

    def columns_of(i):
        return slice(HEAD_DIM + i * side_width, HEAD_DIM + (i + 1) * side_width)

    def span(buf, i):
        return buf.at[:, pl.ds(*spans[i])] if len(buf.shape) == 2 else buf.at[:, :, pl.ds(*spans[i])]

    for j in range(ny):
        eg_part[j, :, :HEAD_DIM] = three_parts(along_of(1 - core, j))
    side_copies = []
    for i in range(2):
        eg_part[:, :, columns_of(i)] = emb_share(1 - core, i).astype(BF16)
        side_copies.append(push(span(eg_part, i), span(eg_side, i), twin))

    pairs = (pairs * (INV_TEMP / norms)).astype(BF16)
    grads = dot_nn(pairs, p_buf[:, :, :width].reshape(passages, width))
    qg_part[...] = grads.astype(BF16).reshape(nz, rows, width)
    one, last, two, other = 1, nz - 1, 2, nz - 2
    far = [push(qg_part.at[zs[4], pl.ds(0, half)], relay_half.at[0], place(zs[other], y, core))]
    far.append(push(qg_part.at[zs[4], pl.ds(half, half)], relay_half.at[1], place(zs[two], y, core)))
    far.append(push(qg_part.at[zs[nz - 3]], relay.at[0], place(zs[last], y, core)))
    far.append(push(qg_part.at[zs[3]], relay.at[1], place(zs[one], y, core)))
    near = [push(qg_part.at[zs[one]], qg_recv.at[0], place(zs[one], y, core))]
    near.append(push(qg_part.at[zs[last]], qg_recv.at[1], place(zs[last], y, core)))
    for i in range(2):
        eg_own[:, :, i * side_width : (i + 1) * side_width] = emb_share(core, i)

    def emb_sum(y_at, i):
        own_part = eg_own[y_at, :, i * side_width : (i + 1) * side_width]
        return own_part + eg_side[y_at, :, columns_of(i)].astype(F32)

    def along_parts(buf, at):
        parts = buf[at, :, :HEAD_DIM].astype(F32)
        return parts[:, 0:1] + parts[:, 1:2] + parts[:, 2:3]

    eg_copies = []
    for i in range(2):
        side_copies[i].wait_recv()
        copies = [None] * ny
        for k in far_first(ny):
            eg_out[k, :, columns_of(i)] = emb_sum(ys[k], i).astype(BF16)
            if i == 0:
                along = along_of(core, ys[k]) + along_parts(eg_side, ys[k])
                eg_out[k, :, :HEAD_DIM] = three_parts(along)
            copies[k] = push(
                span(eg_out.at[k], i), span(eg_recv.at[y], i), place(z, ys[k], core)
            )
        eg_copies.append(copies)
    along = along_of(core, y) + along_parts(eg_side, y)
    slope_copies = []
    slopes = []
    for i in range(2):
        emb_grad = emb_sum(y, i)
        for k in range(1, ny):
            eg_copies[i][k].wait_recv()
            emb_grad = emb_grad + eg_recv[ys[ny - k], :, columns_of(i)].astype(F32)
            if i == 0:
                along = along + along_parts(eg_recv, ys[ny - k])
        part = slice(i * side_width, (i + 1) * side_width)
        residual_grad = (emb_grad - embs[i] * along) / norm
        rgrad_ref[:, part] = residual_grad
        slopes.append(residual_grad.astype(BF16))
        slope_all[x, :, part] = slopes[-1]
        place_at = slope_all.at[:, :, pl.ds(i * side_width, side_width)]
        slope_copies.append(exchange(lambda k: place_at.at[x], place_at))

    save(rgrad_ref, rgrad_hbm)
    for copy in far:
        copy.wait_recv()
    for i, k in enumerate((other, two)):
        total = qg_part[zs[k]].astype(F32) + relay[i].astype(F32)
        extra = relay_half[i].astype(F32)
        parts = [total[:half], total[half:]]
        parts[i] = parts[i] + extra
        relay[i] = jnp.concatenate(parts, axis=0).astype(BF16)
        near.append(push(relay.at[i], qg_recv.at[2 + i], place(zs[k], y, core)))
    upstream = dot_nt(jnp.concatenate(slopes, axis=1), weight[0])
    for i in range(2):
        part = slice(i * side_width, (i + 1) * side_width)
        for k in sorted(range(1, nx), key=lambda k: min(k, nx - k)):
            t = received(slope_copies[i], k)
            upstream = upstream + dot_nt(slope_all[t, :, part], weight[nx - k, :, part])
    up_ref[...] = upstream.astype(BF16)
    save(up_ref, up_hbm)

    query_grad = qg_part[z].astype(F32)
    for i, copy in enumerate(near):
        copy.wait_recv()
        query_grad = query_grad + qg_recv[i].astype(F32)
    qgrad_ref[...] = query_grad
    save(qgrad_ref, qgrad_hbm)
    for copy in sent:
        copy.wait_send()
    for copy in saves:
        copy.wait()


def grouped(source, g, heads):
    first = g * heads
    return jnp.concatenate(
        [source[:, (first + h) * HEAD_DIM : (first + h + 1) * HEAD_DIM] for h in range(heads)],
        axis=0,
    )


def spread(source, groups, heads):
    parts = [grouped(source, g, heads) for g in range(groups)]
    empty = jnp.zeros_like(parts[0])
    lines = [
        jnp.concatenate([part if i == g else empty for i in range(groups)], axis=1)
        for g, part in enumerate(parts)
    ]
    return jnp.concatenate(lines, axis=0)


def backward(
    lastq_ref, up_ref, out_ref, key_ref, value_ref, probs_ref, loss_in, qgrad_in, rgrad_in,
    loss_ref, qgrad_ref, rgrad_ref, lgrad_ref, kgrad_ref, vgrad_ref,
):
    loss_ref[...] = loss_in[...]
    qgrad_ref[...] = qgrad_in[...]
    rgrad_ref[...] = rgrad_in[...]
    rows = lastq_ref.shape[0]
    heads = lastq_ref.shape[1] // HEAD_DIM
    scale = 1.0 / HEAD_DIM**0.5
    up = grouped(up_ref, 0, heads)
    mean = jnp.sum(up.astype(F32) * grouped(out_ref, 0, heads), axis=1, keepdims=True)
    probs = probs_ref[...]
    slopes = dot_nt(up, value_ref[...])
    score_slope = (probs.astype(F32) * (slopes - mean)).astype(BF16)
    vgrad_ref[...] = dot_tn(probs, up).astype(BF16)
    lastq = dot_nn(score_slope, key_ref[...]) * scale
    for h in range(heads):
        lgrad_ref[:, h * HEAD_DIM : (h + 1) * HEAD_DIM] = lastq[h * rows : (h + 1) * rows]
    kgrad_ref[...] = (dot_tn(score_slope, grouped(lastq_ref, 0, heads)) * scale).astype(BF16)


def on_device(
    sizes, last_query, key_cache, value_cache, residual, out_weight, query_emb, lengths, positives
):
    nz, ny, nx = sizes
    rows, width = query_emb.shape
    tokens, kv_width = key_cache.shape
    groups = kv_width // HEAD_DIM
    heads = width // kv_width
    inner = CORES * ny
    passages = inner * rows
    chunk = nz // nx * rows
    wide = width + HEAD_DIM
    vmem = pl.BlockSpec(memory_space=pltpu.VMEM)
    hbm = pl.BlockSpec(memory_space=pl.ANY)
    copies = 3 * (nz - 1) + 7 * ny + 8 * (nx - 1)
    loss, query_grad, residual_grad, upstream, attended, probs = pl.pallas_call(
        functools.partial(kernel, sizes),
        out_shape=(
            jax.ShapeDtypeStruct((1, rows), F32),
            jax.ShapeDtypeStruct((rows, width), F32),
            jax.ShapeDtypeStruct((rows, width), F32),
            jax.ShapeDtypeStruct((rows, width), BF16),
            jax.ShapeDtypeStruct((rows, width), F32),
            jax.ShapeDtypeStruct((groups * heads * rows, tokens), BF16),
        ),
        in_specs=[hbm, hbm, hbm, hbm, hbm, hbm, vmem, vmem],
        out_specs=(hbm,) * 6,
        scratch_shapes=[
            pltpu.VMEM((nz, rows, wide), BF16),
            pltpu.VMEM((inner, rows, wide), BF16),
            pltpu.VMEM((nx, width, width), BF16),
            pltpu.VMEM((tokens, kv_width), BF16),
            pltpu.VMEM((tokens, kv_width), BF16),
            pltpu.VMEM((rows, width), BF16),
            pltpu.VMEM((rows, width), BF16),
            pltpu.VMEM((2, rows, HEAD_DIM), jnp.int32),
            pltpu.VMEM((groups * heads * rows, tokens), F32),
            pltpu.VMEM((groups * heads * rows, tokens), BF16),
            pltpu.VMEM((nx, rows, width), BF16),
            pltpu.VMEM((nx, rows, width), BF16),
            pltpu.VMEM((nx, chunk, passages), F32),
            pltpu.VMEM((nx, chunk, passages), F32),
            pltpu.VMEM((nx, 8, passages), F32),
            pltpu.VMEM((passages, HEAD_DIM), F32),
            pltpu.VMEM((nz, 8, HEAD_DIM), F32),
            pltpu.VMEM((nx, chunk, passages), F32),
            pltpu.VMEM((nx * chunk, passages), BF16),
            pltpu.VMEM((nx, 8, HEAD_DIM), F32),
            pltpu.VMEM((ny, rows, wide), BF16),
            pltpu.VMEM((ny, rows, width), F32),
            pltpu.VMEM((ny, rows, wide), BF16),
            pltpu.VMEM((ny, rows, wide), BF16),
            pltpu.VMEM((ny, rows, wide), BF16),
            pltpu.VMEM((nx, rows, width), BF16),
            pltpu.VMEM((nz, rows, width), BF16),
            pltpu.VMEM((4, rows, width), BF16),
            pltpu.VMEM((2, rows, width), BF16),
            pltpu.VMEM((2, rows // 2, width), BF16),
            pltpu.VMEM((1, rows), F32),
            pltpu.VMEM((rows, width), F32),
            pltpu.VMEM((rows, width), F32),
            pltpu.VMEM((rows, width), BF16),
            pltpu.VMEM((rows, width), F32),
            pltpu.SemaphoreType.DMA((5 + nx,)),
            pltpu.SemaphoreType.DMA((6,)),
            pltpu.SemaphoreType.DMA((copies,)),
            pltpu.SemaphoreType.DMA((copies,)),
        ],
        compiler_params=pltpu.CompilerParams(
            collective_id=0, has_side_effects=True, vmem_limit_bytes=60 * 2**20
        ),
    )(
        last_query, key_cache, value_cache, residual, out_weight, query_emb,
        lengths, positives.reshape(1, rows),
    )
    side = heads * HEAD_DIM
    by_heads = pl.BlockSpec((rows, side), lambda g: (0, g))
    by_group = pl.BlockSpec((tokens, HEAD_DIM), lambda g: (0, g))
    line = pl.BlockSpec((1, rows), lambda g: (0, 0))
    loss, query_grad, residual_grad, lastq_grad, key_grad, value_grad = pl.pallas_call(
        backward,
        grid=(groups,),
        out_shape=(
            jax.ShapeDtypeStruct((1, rows), F32),
            jax.ShapeDtypeStruct((rows, width), F32),
            jax.ShapeDtypeStruct((rows, width), F32),
            jax.ShapeDtypeStruct((rows, width), F32),
            jax.ShapeDtypeStruct((tokens, kv_width), BF16),
            jax.ShapeDtypeStruct((tokens, kv_width), BF16),
        ),
        in_specs=[
            by_heads, by_heads, by_heads, by_group, by_group,
            pl.BlockSpec((heads * rows, tokens), lambda g: (g, 0)),
            line, by_heads, by_heads,
        ],
        out_specs=(line, by_heads, by_heads, by_heads, by_group, by_group),
        compiler_params=pltpu.CompilerParams(vmem_limit_bytes=60 * 2**20),
    )(
        last_query, upstream, attended, key_cache, value_cache, probs, loss, query_grad,
        residual_grad,
    )
    return (loss.reshape(rows), query_grad, residual_grad, lastq_grad, key_grad, value_grad)


def solution(mesh, nz=8, ny=4):
    in_specs = (
        P("dp", "mp"),
        P("dp", "mp"),
        P("dp", "mp"),
        P("dp", "mp"),
        P("mp", None),
        P("dp", "mp"),
        P("dp", None),
        P("dp"),
    )
    out_specs = (P("dp"), P("dp", "mp"), P("dp", "mp"), P("dp", "mp"), P("dp", "mp"), P("dp", "mp"))
    sizes = (nz, ny, mesh.shape["mp"])
    return jax.shard_map(
        functools.partial(on_device, sizes),
        mesh=mesh,
        in_specs=in_specs,
        out_specs=out_specs,
        check_vma=False,
    )
```

profile of v0, /device:TPU:1, one launch (start us, length us, event | category | flops | bytes accessed | tf_op | source)
XLA Modules:
  0.0 57.4 jit_solution(15089355917263691039)
XLA Ops:
  0.6 52.6 %shard_map.127 = (f32[1,32]{1,0:T(1,128)}, f32[32,1024]{1,0:T(8,128)}, f32[32,1024]{1,0:T(8,128)}, bf16[32,1024]{1,0:T(8,128)(2,1)}, f32[32,1024]{1,0:T(8,128)}, /*index=5*/bf16[256,2048]{1,0:T(8,128)(2,1)}) custom-call(bf16[32,1024]{1,0:T(8,128)(2,1)} %lastq_ref.1, bf16[2048,256]{1,0:T(8,128)(2,1)} %key_ref.1, bf16[2048,256]{1,0:T(8,128)(2,1)} %value_ref.1, ...), custom_call_target="tpu_custom_call" | custom-call | tf_op jit(solution)/shard_map/pallas_call | solution.py:484
  53.3 4.1 %shard_map.128 = (f32[1,32]{1,0:T(1,128)}, f32[32,1024]{1,0:T(8,128)}, f32[32,1024]{1,0:T(8,128)}, f32[32,1024]{1,0:T(8,128)}, bf16[2048,256]{1,0:T(8,128)(2,1)}, /*index=5*/bf16[2048,256]{1,0:T(8,128)(2,1)}) custom-call(bf16[32,1024]{1,0:T(8,128)(2,1)} %lastq_ref.1, bf16[32,1024]{1,0:T(8,128)(2,1)} %get-tuple-element.18.up_ref, ...), custom_call_target="tpu_custom_call" | custom-call | tf_op jit(solution)/shard_map/pallas_call | solution.py:548
where the time goes:
time: 57.5 us; the launch traced here: 57.4 us
  Pallas kernels  56.7 us (99%)
  between operations  0.64 us (1%)
    pallas_call x1, Pallas kernels, on_device(): pl.pallas_call(functools.partial(kernel, sizes), out_shape=(jax.ShapeDtyp...  52.6 us
    pallas_call x1, Pallas kernels, on_device(): pl.pallas_call(backward, grid=(groups,), out_shape=(jax.ShapeDtypeStruct(...  4.07 us

commit v1 on v0

--- a/solution.py
+++ b/solution.py
@@ -70,10 +70,6 @@
     partners = [place(t, y, core) for t in zs[1:]] + [place(z, t, core) for t in ys[1:]]
     partners += [twin] + [{"mp": t} for t in xs[1:]]
 
-    barrier = pltpu.get_barrier_semaphore()
-    for partner in partners:
-        pl.semaphore_signal(barrier, inc=1, device_id=partner, device_id_type=MESH)
-
     loads = [
         pltpu.make_async_copy(query_hbm, q_buf.at[z, :, pl.ds(0, width)], load_sem.at[0]),
         pltpu.make_async_copy(lastq_hbm, lastq, load_sem.at[1]),
@@ -90,6 +86,10 @@
         )
     for load in loads[:4]:
         load.start()
+
+    barrier = pltpu.get_barrier_semaphore()
+    for partner in partners:
+        pl.semaphore_signal(barrier, inc=1, device_id=partner, device_id_type=MESH)
 
     saves = []
 
@@ -275,8 +275,6 @@
     for k in range(1, nx):
         scores = scores + s_recv[received(s_copies, k)]
     scores = scores * (INV_TEMP / norms)
-    s_all[x] = scores
-    all_copies = exchange(lambda k: s_all.at[x], s_all)
 
     top = jnp.max(scores, axis=1, keepdims=True)
     total = jnp.sum(jnp.exp(scores - top), axis=1, keepdims=True)
@@ -288,6 +286,8 @@
     columns = jnp.where(chunk_lane == 0, top, jnp.where(chunk_lane == 1, total, hit))
     stat[z] = jnp.concatenate([columns] * (HEAD_DIM // chunk), axis=0).T[:8]
     stat_copies = [push(stat.at[z], stat.at[z], place(zs[k], y, core)) for k in far_first(nz)]
+    s_all[x] = scores
+    all_copies = exchange(lambda k: s_all.at[x], s_all)
     for copy in stat_copies:
         copy.wait_recv()
     every = stat[...]

time: 57.5 us -> 57.4 us (level)
  no operation moved by 1% of the time
where the time goes in v1:
time: 57.4 us; the launch traced here: 57.3 us
  Pallas kernels  56.7 us (99%)
  between operations  0.64 us (1%)
    pallas_call x1, Pallas kernels, on_device(): pl.pallas_call(functools.partial(kernel, sizes), out_shape=(jax.ShapeDtyp...  52.6 us
    pallas_call x1, Pallas kernels, on_device(): pl.pallas_call(backward, grid=(groups,), out_shape=(jax.ShapeDtypeStruct(...  4.07 us

profile of v1, /device:TPU:1, one launch (start us, length us, event | category | flops | bytes accessed | tf_op | source)
XLA Modules:
  0.0 57.3 jit_solution(11770123457713275461)
XLA Ops:
  0.6 52.6 %shard_map.127 = (f32[1,32]{1,0:T(1,128)}, f32[32,1024]{1,0:T(8,128)}, f32[32,1024]{1,0:T(8,128)}, bf16[32,1024]{1,0:T(8,128)(2,1)}, f32[32,1024]{1,0:T(8,128)}, /*index=5*/bf16[256,2048]{1,0:T(8,128)(2,1)}) custom-call(bf16[32,1024]{1,0:T(8,128)(2,1)} %lastq_ref.1, bf16[2048,256]{1,0:T(8,128)(2,1)} %key_ref.1, bf16[2048,256]{1,0:T(8,128)(2,1)} %value_ref.1, ...), custom_call_target="tpu_custom_call" | custom-call | tf_op jit(solution)/shard_map/pallas_call | solution.py:484
  53.2 4.1 %shard_map.128 = (f32[1,32]{1,0:T(1,128)}, f32[32,1024]{1,0:T(8,128)}, f32[32,1024]{1,0:T(8,128)}, f32[32,1024]{1,0:T(8,128)}, bf16[2048,256]{1,0:T(8,128)(2,1)}, /*index=5*/bf16[2048,256]{1,0:T(8,128)(2,1)}) custom-call(bf16[32,1024]{1,0:T(8,128)(2,1)} %lastq_ref.1, bf16[32,1024]{1,0:T(8,128)(2,1)} %get-tuple-element.18.up_ref, ...), custom_call_target="tpu_custom_call" | custom-call | tf_op jit(solution)/shard_map/pallas_call | solution.py:548

commit v2 on v1

--- a/solution.py
+++ b/solution.py
@@ -378,6 +378,17 @@
             )
         eg_copies.append(copies)
     along = along_of(core, y) + along_parts(eg_side, y)
+    def pass_on():
+        for copy in far:
+            copy.wait_recv()
+        for i, k in enumerate((other, two)):
+            total = qg_part[zs[k]].astype(F32) + relay[i].astype(F32)
+            extra = relay_half[i].astype(F32)
+            parts = [total[:half], total[half:]]
+            parts[i] = parts[i] + extra
+            relay[i] = jnp.concatenate(parts, axis=0).astype(BF16)
+            near.append(push(relay.at[i], qg_recv.at[2 + i], place(zs[k], y, core)))
+
     slope_copies = []
     slopes = []
     for i in range(2):
@@ -394,17 +405,10 @@
         slope_all[x, :, part] = slopes[-1]
         place_at = slope_all.at[:, :, pl.ds(i * side_width, side_width)]
         slope_copies.append(exchange(lambda k: place_at.at[x], place_at))
+        if i == 0:
+            pass_on()
 
     save(rgrad_ref, rgrad_hbm)
-    for copy in far:
-        copy.wait_recv()
-    for i, k in enumerate((other, two)):
-        total = qg_part[zs[k]].astype(F32) + relay[i].astype(F32)
-        extra = relay_half[i].astype(F32)
-        parts = [total[:half], total[half:]]
-        parts[i] = parts[i] + extra
-        relay[i] = jnp.concatenate(parts, axis=0).astype(BF16)
-        near.append(push(relay.at[i], qg_recv.at[2 + i], place(zs[k], y, core)))
     upstream = dot_nt(jnp.concatenate(slopes, axis=1), weight[0])
     for i in range(2):
         part = slice(i * side_width, (i + 1) * side_width)

time: 57.4 us -> 57.4 us (level)
  no operation moved by 1% of the time
where the time goes in v2:
time: 57.4 us; the launch traced here: 57.3 us
  Pallas kernels  56.7 us (99%)
  between operations  0.64 us (1%)
    pallas_call x1, Pallas kernels, on_device(): pl.pallas_call(functools.partial(kernel, sizes), out_shape=(jax.ShapeDtyp...  52.6 us
    pallas_call x1, Pallas kernels, on_device(): pl.pallas_call(backward, grid=(groups,), out_shape=(jax.ShapeDtypeStruct(...  4.07 us

profile of v2, /device:TPU:1, one launch (start us, length us, event | category | flops | bytes accessed | tf_op | source)
XLA Modules:
  0.0 57.3 jit_solution(10667540348612933933)
XLA Ops:
  0.6 52.6 %shard_map.127 = (f32[1,32]{1,0:T(1,128)}, f32[32,1024]{1,0:T(8,128)}, f32[32,1024]{1,0:T(8,128)}, bf16[32,1024]{1,0:T(8,128)(2,1)}, f32[32,1024]{1,0:T(8,128)}, /*index=5*/bf16[256,2048]{1,0:T(8,128)(2,1)}) custom-call(bf16[32,1024]{1,0:T(8,128)(2,1)} %lastq_ref.1, bf16[2048,256]{1,0:T(8,128)(2,1)} %key_ref.1, bf16[2048,256]{1,0:T(8,128)(2,1)} %value_ref.1, ...), custom_call_target="tpu_custom_call" | custom-call | tf_op jit(solution)/shard_map/pallas_call | solution.py:488
  53.2 4.1 %shard_map.128 = (f32[1,32]{1,0:T(1,128)}, f32[32,1024]{1,0:T(8,128)}, f32[32,1024]{1,0:T(8,128)}, f32[32,1024]{1,0:T(8,128)}, bf16[2048,256]{1,0:T(8,128)(2,1)}, /*index=5*/bf16[2048,256]{1,0:T(8,128)(2,1)}) custom-call(bf16[32,1024]{1,0:T(8,128)(2,1)} %lastq_ref.1, bf16[32,1024]{1,0:T(8,128)(2,1)} %get-tuple-element.18.up_ref, ...), custom_call_target="tpu_custom_call" | custom-call | tf_op jit(solution)/shard_map/pallas_call | solution.py:552
